TPU v7x, 256 devices: a whole 4x4x8 slice. The times are simulated.
256 devices in a mesh: inner: 16 (over x, z_lo, core), outer: 16 (over y, z_hi).
Axes of the slice: x: 4, y: 4, z: 8 (z_hi: 4, z_lo: 2; z = z_hi * 2 + z_lo), core: 2. Of those that a mesh axis runs over, the one named last changes fastest.
Arguments:
- queries: bfloat16 [65536, 3072], P(('inner', 'outer')), may hold values from -30 to 30
- keys: bfloat16 [65536, 3072], P(('inner', 'outer')), may hold values from -30 to 30
- values: bfloat16 [65536, 3072], P(('inner', 'outer')), may hold values from -6 to 6
- frame_mask: int32 [512, 30], P(('inner', 'outer')), may hold values from 0 to 1, as said below
- query_order: int32 [512], P(('inner', 'outer')), may hold values from 0 to 511, as said below
Outputs:
- attended: bfloat16 [65536, 3072], P(('inner', 'outer'))
Inputs may be any that keep to these rules, and one draw needn't show every extreme that they name: query_order[b] // 2 == b // 2: each device's blocks take that device's mask rows in some order. `frame_mask`: entries naming a device outside the clip are 0; for each row r, the entry at offsets 0 and slot r % 2 is 1, so every query block has at least one live key block on its own device.
All inputs are finite; a program needn't handle non-finite values.
Results may differ from a plain program's by a relative error of at most 0.0056.
Values may be sent and summed in bfloat16 or wider, within the bound.
A program may use at most 128 MiB of HBM per device.

v0:
```python
import math

import jax
import jax.numpy as jnp
from jax import lax
from jax.sharding import PartitionSpec as P

HEADS = 24


def passed_along(block, axis, distance):
    devices = range(lax.axis_size(axis))
    route = [(i - distance, i) for i in devices if i - distance in devices]
    return lax.ppermute(block, axis, route)


def attend(qrows, live, window):
    tok = qrows.shape[0]
    dim = qrows.shape[1]
    size = dim // HEADS
    blocks = live.shape[0]
    width = window.shape[1]
    group = math.gcd(HEADS, 4)
    count = HEADS // group
    grid = jnp.repeat(
        jnp.repeat(live.reshape(blocks, -1) > 0, tok // blocks, axis=0), tok // blocks, axis=1
    )
    query = qrows.reshape(tok, count, group, size).transpose(1, 0, 2, 3)
    keyset = window[0].reshape(width, count, group, size).transpose(1, 0, 2, 3)
    valset = window[1].reshape(width, count, group, size).transpose(1, 0, 2, 3)

    def one_group(operands):
        qpart, kpart, vpart = operands
        score = jnp.einsum(
            "qhd,khd->hqk", qpart, kpart, preferred_element_type=jnp.float32
        ) * size ** (-0.5)
        top = jnp.max(jnp.where(grid[None], score, -1e30), axis=-1)
        prob = jnp.exp(jnp.where(grid[None], score - top[..., None], -1e30))
        total = jnp.sum(prob, axis=-1)
        numer = jnp.einsum(
            "hqk,khd->qhd", prob.astype(jnp.bfloat16), vpart, preferred_element_type=jnp.float32
        )
        scaled = (numer / jnp.maximum(total.T, 1.0)[..., None]).astype(jnp.bfloat16)
        return (scaled, top, total)

    scaled, top, total = lax.map(one_group, (query, keyset, valset))
    scaled = scaled.transpose(1, 0, 2, 3).reshape(tok, dim)
    top = top.transpose(2, 0, 1).reshape(tok, HEADS)
    total = total.transpose(2, 0, 1).reshape(tok, HEADS)
    return (scaled, top, total)


def combine(parts):
    tops = jnp.stack([p[1] for p in parts])
    totals = jnp.stack([p[2] for p in parts])
    partial_set = jnp.stack([p[0] for p in parts])
    tok = partial_set.shape[1]
    dim = partial_set.shape[2]
    best = jnp.max(tops, axis=0)
    weight = jnp.exp(tops - best[None]) * totals
    denom = jnp.sum(weight, axis=0)
    numer = jnp.sum(
        weight[..., None] * partial_set.reshape(3, tok, HEADS, dim // HEADS).astype(jnp.float32),
        axis=0,
    )
    return (numer / denom[..., None]).reshape(tok, dim).astype(jnp.bfloat16)


def shards(queries, keys, values, frame_mask, query_order):
    blocks = frame_mask.shape[0]
    outer_count = lax.axis_size("outer")
    place = lax.axis_index("outer")
    device = lax.axis_index("inner") * outer_count + place
    local_rows = query_order - device * blocks
    live = frame_mask[local_rows].reshape(blocks, 5, 3, blocks)
    pair = jnp.stack([keys, values])
    behind = []
    moving = pair
    for step in range(2):
        moving = passed_along(moving, "inner", 1)
        behind.append(moving)
    ahead = []
    moving = pair
    for step in range(2):
        moving = passed_along(moving, "inner", -1)
        ahead.append(moving)
    frames = [behind[1], behind[0], pair, ahead[0], ahead[1]]
    window = jnp.concatenate(frames, axis=1)
    parts = [attend(queries, live[:, :, 1, :], window)]
    for reach in (1, -1):
        sent_rows = live[:, :, 1 + reach, :].astype(jnp.bfloat16)
        far_query, far_live = passed_along((queries, sent_rows), "outer", reach)
        scaled, top, total = attend(far_query, far_live, window)
        scaled = passed_along(scaled, "outer", -reach)
        top, total = passed_along((top, total), "outer", -reach)
        outside = (place + reach < 0) | (place + reach >= outer_count)
        top = jnp.where(outside, jnp.float32(-1e30), top)
        parts.append((scaled, top, total))
    return combine(parts)


def solution(mesh):
    placed = (
        P(("inner", "outer"), None),
        P(("inner", "outer"), None),
        P(("inner", "outer"), None),
        P(("inner", "outer"), None),
        P(("inner", "outer")),
    )
    return jax.shard_map(
        shards, mesh=mesh, in_specs=placed, out_specs=P(("inner", "outer"), None), check_vma=False
    )
```

profile of v0, /device:TPU:26, one launch (start us, length us, event | category | flops | bytes accessed | tf_op | source)
XLA Modules:
  0.0 444.1 jit_solution(5501764738145776525)
XLA Ops:
  7.3 4.5 %collective-permute-start.2 = (bf16[2,256,3072]{1,2,0:T(8,128)(2,1)}, bf16[2,256,3072]{1,2,0:T(8,128)(2,1)}, u32[]{:S(2)}, u32[]{:S(2)}) collective-permute-start(bf16[2,256,3072]{1,2,0:T(8,128)(2,1)} %pad_maximum_fusion), channel_id=1, source_target_pairs={{16,0},{32,16},{48,32},{64,48},{80,64},{96,80},{112,96},{128,112},... | collective-permute-start | bytes 9437192 | tf_op jit(solution)/shard_map/ppermute | solution.py:14
  11.8 97.5 %collective-permute-done = bf16[2,256,3072]{1,2,0:T(8,128)(2,1)} collective-permute-done((bf16[2,256,3072]{1,2,0:T(8,128)(2,1)}, bf16[2,256,3072]{1,2,0:T(8,128)(2,1)}, u32[]{:S(2)}, u32[]{:S(2)}) %collective-permute-start) | collective-permute-done | bytes 3145760 | tf_op jit(solution)/shard_map/ppermute | solution.py:14
  113.8 5.2 %collective-permute-start.5 = (bf16[256,3072]{0,1:T(8,128)(2,1)}, bf16[256,3072]{0,1:T(8,128)(2,1)}, u32[]{:S(2)}, u32[]{:S(2)}) collective-permute-start(bf16[256,3072]{0,1:T(8,128)(2,1)} %copy.58), channel_id=1, source_target_pairs={{0,1},{1,2},{2,3},{3,4},{4,5},{5,6},{6,7},{7,8},{8,9},{9,10},{10,1... | collective-permute-start | bytes 4718600 | tf_op jit(solution)/shard_map/ppermute | solution.py:14
  119.0 6.0 %collective-permute-start.8 = (bf16[256,3072]{0,1:T(8,128)(2,1)}, bf16[256,3072]{0,1:T(8,128)(2,1)}, u32[]{:S(2)}, u32[]{:S(2)}) collective-permute-start(bf16[256,3072]{0,1:T(8,128)(2,1)} %copy.58), channel_id=1, source_target_pairs={{1,0},{2,1},{3,2},{4,3},{5,4},{6,5},{7,6},{8,7},{9,8},{10,9},{11,1... | collective-permute-start | bytes 4718600 | tf_op jit(solution)/shard_map/ppermute | solution.py:14
  125.1 4.3 collective-permute-start.3
  130.2 3.2 collective-permute-start.4
  133.8 85.4 %collective-permute-done.4 = bf16[2,5,2]{1,2,0:T(2,128)(2,1)S(1)} collective-permute-done((bf16[2,5,2]{1,2,0:T(2,128)(2,1)S(1)}, bf16[2,5,2]{1,2,0:T(2,128)(2,1)S(1)}, u32[]{:S(2)}, u32[]{:S(2)}) %collective-permute-start.4) | collective-permute-done | bytes 72 | tf_op jit(solution)/shard_map/ppermute | solution.py:14
  219.2 3.3 collective-permute-start.7
  234.4 5.9 %fusion.133 = (bf16[1,1280,3072]{1,2,0:T(8,128)(2,1)}, bf16[1,1280,3072]{1,2,0:T(8,128)(2,1)}) fusion(bf16[2,1280,3072]{1,2,0:T(8,128)(2,1)S(1)} %constant_dynamic-update-slice_fusion), kind=kLoop, calls=%fused_computation.102 | loop fusion | bytes 31457280 | tf_op jit(solution)/shard_map/slice | solution.py:29
  240.3 10.6 %copy.61 = bf16[6,1280,4,128]{3,1,2,0:T(8,128)(2,1)} copy(bf16[6,1280,4,128]{1,3,2,0:T(8,128)(2,1)} %bitcast.265) | data formatting | bytes 15728640
  252.3 52.3 %while.46 = (s32[]{:T(128)}, bf16[6,256,4,128]{1,3,2,0:T(8,128)(2,1)}, f32[6,4,256]{2,1,0:T(4,128)S(1)}, f32[6,4,256]{2,1,0:T(4,128)S(1)}, bf16[6,1280,4,128]{1,...) while((s32[]{:T(128)}, ...), condition=%wide.region_7.8_spmd.clone, body=%wide.region_4.7_spmd.clone.sunk | while | flops 685767680 | bytes 20890208 | solution.py:46
  257.4 3.7 fusion.154
  261.7 2.8 select_reduce_fusion.7
  266.1 3.6 fusion.154
  270.4 2.8 select_reduce_fusion.7
  274.8 3.7 fusion.154
  279.1 2.8 select_reduce_fusion.7
  283.5 3.7 fusion.154
  287.8 2.8 select_reduce_fusion.7
  292.3 3.6 fusion.154
  301.0 3.6 fusion.154
  304.6 5.7 %collective-permute-start.6 = (f32[256,24]{0,1:T(8,128)S(1)}, f32[256,24]{0,1:T(8,128)S(1)}, u32[]{:S(2)}, u32[]{:S(2)}) collective-permute-start(f32[256,24]{0,1:T(8,128)S(1)} %reshape.140), channel_id=1, source_target_pairs={{1,0},{2,1},{3,2},{4,3},{5,4},{6,5},{7,6},{8,7},{9,8},{10,9},{11,1... | collective-permute-start | bytes 73736 | tf_op jit(solution)/shard_map/ppermute | solution.py:14
  311.6 52.3 %while.47 = (s32[]{:T(128)}, bf16[6,256,4,128]{1,3,2,0:T(8,128)(2,1)}, f32[6,4,256]{2,1,0:T(4,128)S(1)}, f32[6,4,256]{2,1,0:T(4,128)S(1)}, bf16[6,1280,4,128]{1,...) while((s32[]{:T(128)}, ...), condition=%wide.region_11.12_spmd.clone, body=%wide.region_8.11_spmd.clone.sunk | while | flops 685767680 | bytes 20890208 | solution.py:46
  312.2 2.8 select_reduce_fusion.8
  316.7 3.6 fusion.158
  325.4 3.6 fusion.158
  329.6 2.8 select_reduce_fusion.8
  334.1 3.6 fusion.158
  338.3 2.8 select_reduce_fusion.8
  342.8 3.7 fusion.158
  347.1 2.8 select_reduce_fusion.8
  351.5 3.7 fusion.158
  355.8 2.8 select_reduce_fusion.8
  360.2 3.7 fusion.158
  365.8 6.9 %collective-permute-start.12 = (bf16[256,3072]{0,1:T(8,128)(2,1)}, bf16[256,3072]{0,1:T(8,128)(2,1)}, u32[]{:S(2)}, u32[]{:S(2)}) collective-permute-start(bf16[256,3072]{0,1:T(8,128)(2,1)} %bitcast.29), channel_id=1, source_target_pairs={{1,0},{2,1},{3,2},{4,3},{5,4},{6,5},{7,6},{8,7},{9,8},{10,9},{11,1... | collective-permute-start | bytes 4718600 | tf_op jit(solution)/shard_map/ppermute | solution.py:14
  374.9 48.1 %while.45 = (s32[]{:T(128)}, bf16[6,256,4,128]{1,3,2,0:T(8,128)(2,1)S(1)}, f32[6,4,256]{2,1,0:T(4,128)S(1)}, f32[6,4,256]{2,1,0:T(4,128)S(1)}, bf16[6,1280,4,128...) while((s32[]{:T(128)}, ...), condition=%wide.region_3.4_spmd.clone, body=%wide.region_0.3_spmd.clone.sunk | while | flops 685767680 | bytes 20890208 | solution.py:46
  375.5 2.8 select_reduce_fusion.6
  380.0 2.9 fusion.150
  388.0 2.9 fusion.150
  391.5 2.8 select_reduce_fusion.6
  396.0 2.9 fusion.150
  404.0 2.9 fusion.150
  407.6 2.8 select_reduce_fusion.6
  412.0 2.9 fusion.150
  420.1 2.9 fusion.150
  423.1 6.9 %collective-permute-start.10 = (f32[256,24]{0,1:T(8,128)S(1)}, f32[256,24]{0,1:T(8,128)S(1)}, u32[]{:S(2)}, u32[]{:S(2)}) collective-permute-start(f32[256,24]{0,1:T(8,128)S(1)} %reshape.144), channel_id=1, source_target_pairs={{1,0},{2,1},{3,2},{4,3},{5,4},{6,5},{7,6},{8,7},{9,8},{10,9},{11,1... | collective-permute-start | bytes 73736 | tf_op jit(solution)/shard_map/ppermute | solution.py:14
  432.0 6.8 %collective-permute-done.11 = f32[256,24]{0,1:T(8,128)S(1)} collective-permute-done((f32[256,24]{0,1:T(8,128)S(1)}, f32[256,24]{0,1:T(8,128)S(1)}, u32[]{:S(2)}, u32[]{:S(2)}) %collective-permute-start.11) | collective-permute-done | bytes 24608 | tf_op jit(solution)/shard_map/ppermute | solution.py:14
  438.8 3.1 multiply_reduce_fusion
  (173 shorter events, 93.3 us)
Async XLA Ops:
  0.0 129.4 %copy-start = (s32[2,30]{1,0:T(2,128)S(1)}, s32[2,30]{1,0:T(2,128)}, u32[]{:S(2)}) copy-start(s32[2,30]{1,0:T(2,128)} %param.14) | copy-start | bytes 724
  3.4 121.6 %copy-start.2 = (s32[2]{0:T(128)S(1)}, s32[2]{0:T(128)}, u32[]{:S(2)}) copy-start(s32[2]{0:T(128)} %param.15) | copy-start | bytes 28
  5.4 103.9 %collective-permute-start = (bf16[2,256,3072]{1,2,0:T(8,128)(2,1)}, bf16[2,256,3072]{1,2,0:T(8,128)(2,1)}, u32[]{:S(2)}, u32[]{:S(2)}) collective-permute-start(bf16[2,256,3072]{1,2,0:T(8,128)(2,1)} %pad_maximum_fusion), channel_id=1, source_target_pairs={{0,16},{16,32},{32,48},{48,64},{64,80},{80,96},{96,112},{112,128},... | collective-permute-start | bytes 9437192 | tf_op jit(solution)/shard_map/ppermute | solution.py:14
  7.3 117.8 %collective-permute-start.2 = (bf16[2,256,3072]{1,2,0:T(8,128)(2,1)}, bf16[2,256,3072]{1,2,0:T(8,128)(2,1)}, u32[]{:S(2)}, u32[]{:S(2)}) collective-permute-start(bf16[2,256,3072]{1,2,0:T(8,128)(2,1)} %pad_maximum_fusion), channel_id=1, source_target_pairs={{16,0},{32,16},{48,32},{64,48},{80,64},{96,80},{112,96},{128,112},... | collective-permute-start | bytes 9437192 | tf_op jit(solution)/shard_map/ppermute | solution.py:14
  109.3 116.5 %collective-permute-start.1 = (bf16[2,256,3072]{1,2,0:T(8,128)(2,1)}, bf16[2,256,3072]{1,2,0:T(8,128)(2,1)}, u32[]{:S(2)}, u32[]{:S(2)}) collective-permute-start(bf16[2,256,3072]{1,2,0:T(8,128)(2,1)} %collective-permute-done), channel_id=1, source_target_pairs={{0,16},{16,32},{32,48},{48,64},{64,80},{80,96},{96,112},{112,128},... | collective-permute-start | bytes 9437192 | tf_op jit(solution)/shard_map/ppermute | solution.py:14
  113.8 137.1 %collective-permute-start.5 = (bf16[256,3072]{0,1:T(8,128)(2,1)}, bf16[256,3072]{0,1:T(8,128)(2,1)}, u32[]{:S(2)}, u32[]{:S(2)}) collective-permute-start(bf16[256,3072]{0,1:T(8,128)(2,1)} %copy.58), channel_id=1, source_target_pairs={{0,1},{1,2},{2,3},{3,4},{4,5},{5,6},{6,7},{7,8},{8,9},{9,10},{10,1... | collective-permute-start | bytes 4718600 | tf_op jit(solution)/shard_map/ppermute | solution.py:14
  119.0 191.3 %collective-permute-start.8 = (bf16[256,3072]{0,1:T(8,128)(2,1)}, bf16[256,3072]{0,1:T(8,128)(2,1)}, u32[]{:S(2)}, u32[]{:S(2)}) collective-permute-start(bf16[256,3072]{0,1:T(8,128)(2,1)} %copy.58), channel_id=1, source_target_pairs={{1,0},{2,1},{3,2},{4,3},{5,4},{6,5},{7,6},{8,7},{9,8},{10,9},{11,1... | collective-permute-start | bytes 4718600 | tf_op jit(solution)/shard_map/ppermute | solution.py:14
  125.1 107.2 %collective-permute-start.3 = (bf16[2,256,3072]{1,2,0:T(8,128)(2,1)}, bf16[2,256,3072]{1,2,0:T(8,128)(2,1)}, u32[]{:S(2)}, u32[]{:S(2)}) collective-permute-start(bf16[2,256,3072]{1,2,0:T(8,128)(2,1)} %collective-permute-done.2), channel_id=1, source_target_pairs={{16,0},{32,16},{48,32},{64,48},{80,64},{96,80},{112,96},{128,112},... | collective-permute-start | bytes 9437192 | tf_op jit(solution)/shard_map/ppermute | solution.py:14
  130.2 89.0 %collective-permute-start.4 = (bf16[2,5,2]{1,2,0:T(2,128)(2,1)S(1)}, bf16[2,5,2]{1,2,0:T(2,128)(2,1)S(1)}, u32[]{:S(2)}, u32[]{:S(2)}) collective-permute-start(bf16[2,5,2]{1,2,0:T(2,128)(2,1)S(1)} %bitcast.289), channel_id=1, source_target_pairs={{0,1},{1,2},{2,3},{3,4},{4,5},{5,6},{6,7},{7,8},{8,9},{9,10},{10,1... | collective-permute-start | bytes 128 | tf_op jit(solution)/shard_map/ppermute | solution.py:14
  219.2 6.3 %collective-permute-start.7 = (bf16[2,5,2]{1,2,0:T(2,128)(2,1)S(1)}, bf16[2,5,2]{1,2,0:T(2,128)(2,1)S(1)}, u32[]{:S(2)}, u32[]{:S(2)}) collective-permute-start(bf16[2,5,2]{1,2,0:T(2,128)(2,1)S(1)} %bitcast.290), channel_id=1, source_target_pairs={{1,0},{2,1},{3,2},{4,3},{5,4},{6,5},{7,6},{8,7},{9,8},{10,9},{11,1... | collective-permute-start | bytes 128 | tf_op jit(solution)/shard_map/ppermute | solution.py:14
  304.6 125.4 %collective-permute-start.6 = (f32[256,24]{0,1:T(8,128)S(1)}, f32[256,24]{0,1:T(8,128)S(1)}, u32[]{:S(2)}, u32[]{:S(2)}) collective-permute-start(f32[256,24]{0,1:T(8,128)S(1)} %reshape.140), channel_id=1, source_target_pairs={{1,0},{2,1},{3,2},{4,3},{5,4},{6,5},{7,6},{8,7},{9,8},{10,9},{11,1... | collective-permute-start | bytes 73736 | tf_op jit(solution)/shard_map/ppermute | solution.py:14
  363.9 68.1 %collective-permute-start.9 = (f32[256,24]{0,1:T(8,128)S(1)}, f32[256,24]{0,1:T(8,128)S(1)}, u32[]{:S(2)}, u32[]{:S(2)}) collective-permute-start(f32[256,24]{0,1:T(8,128)S(1)} %reshape.143), channel_id=1, source_target_pairs={{0,1},{1,2},{2,3},{3,4},{4,5},{5,6},{6,7},{7,8},{8,9},{9,10},{10,1... | collective-permute-start | bytes 73736 | tf_op jit(solution)/shard_map/ppermute | solution.py:14
  365.8 73.0 %collective-permute-start.12 = (bf16[256,3072]{0,1:T(8,128)(2,1)}, bf16[256,3072]{0,1:T(8,128)(2,1)}, u32[]{:S(2)}, u32[]{:S(2)}) collective-permute-start(bf16[256,3072]{0,1:T(8,128)(2,1)} %bitcast.29), channel_id=1, source_target_pairs={{1,0},{2,1},{3,2},{4,3},{5,4},{6,5},{7,6},{8,7},{9,8},{10,9},{11,1... | collective-permute-start | bytes 4718600 | tf_op jit(solution)/shard_map/ppermute | solution.py:14
  372.8 66.1 %collective-permute-start.13 = (bf16[256,3072]{0,1:T(8,128)(2,1)}, bf16[256,3072]{0,1:T(8,128)(2,1)}, u32[]{:S(2)}, u32[]{:S(2)}) collective-permute-start(bf16[256,3072]{0,1:T(8,128)(2,1)} %bitcast.32), channel_id=1, source_target_pairs={{0,1},{1,2},{2,3},{3,4},{4,5},{5,6},{6,7},{7,8},{8,9},{9,10},{10,1... | collective-permute-start | bytes 4718600 | tf_op jit(solution)/shard_map/ppermute | solution.py:14
  423.1 8.9 %collective-permute-start.10 = (f32[256,24]{0,1:T(8,128)S(1)}, f32[256,24]{0,1:T(8,128)S(1)}, u32[]{:S(2)}, u32[]{:S(2)}) collective-permute-start(f32[256,24]{0,1:T(8,128)S(1)} %reshape.144), channel_id=1, source_target_pairs={{1,0},{2,1},{3,2},{4,3},{5,4},{6,5},{7,6},{8,7},{9,8},{10,9},{11,1... | collective-permute-start | bytes 73736 | tf_op jit(solution)/shard_map/ppermute | solution.py:14
  430.1 8.7 %collective-permute-start.11 = (f32[256,24]{0,1:T(8,128)S(1)}, f32[256,24]{0,1:T(8,128)S(1)}, u32[]{:S(2)}, u32[]{:S(2)}) collective-permute-start(f32[256,24]{0,1:T(8,128)S(1)} %reshape.145), channel_id=1, source_target_pairs={{0,1},{1,2},{2,3},{3,4},{4,5},{5,6},{6,7},{7,8},{8,9},{9,10},{10,1... | collective-permute-start | bytes 73736 | tf_op jit(solution)/shard_map/ppermute | solution.py:14
  438.8 5.3 %copy-start.1 = (s32[2,30]{1,0:T(2,128)S(1)}, s32[2,30]{1,0:T(2,128)}, u32[]{:S(2)}) copy-start(s32[2,30]{1,0:T(2,128)} %param.14) | copy-start | bytes 724
where the time goes:
time: 446 us; the launch traced here: 444 us
  waiting for transfers between devices  192 us (43%)
  matrix products  111 us (25%)
  starting transfers between devices  55.6 us (12%)
  local copies, waits for them, and re-layouts  48.1 us (11%)
  other arithmetic  35.9 us (8%)
    ppermute x14, waiting for transfers between devices, passed_along(): return lax.ppermute(block, axis, route)  192 us
    dot_general x18, matrix products, one_group(): jnp.einsum('hqk,khd->qhd', prob.astype(jnp.bfloat16), vpart, preferred_el...  61.5 us
    ppermute x14, starting transfers between devices, passed_along(): return lax.ppermute(block, axis, route)  55.6 us
    dot_general x18, matrix products, one_group(): jnp.einsum('qhd,khd->hqk', qpart, kpart, preferred_element_type=jnp.float32)  49.7 us
    reduce_sum x18, other arithmetic, one_group(): total = jnp.sum(prob, axis=-1)  30.1 us
    unnamed x22, local copies, waits for them, and re-layouts  23.3 us
    broadcast_in_dim x18, local copies, waits for them, and re-layouts, one_group(): prob = jnp.exp(jnp.where(grid[None], score - top[..., None], -1e+30))  8.99 us
  transfers between devices with their start and end apart: 14, of which 4 were waited for; matrix products, arithmetic and copies ran while one was open for 42% of the time, Pallas kernels for 0%

commit v1 on v0

v1 whole, which is shorter than its diff:
```python
import math

import jax
import jax.numpy as jnp
from jax import lax
from jax.experimental import pallas as pl
from jax.experimental.pallas import tpu as pltpu
from jax.sharding import PartitionSpec as P

HEADS = 24
SIZE = 128
RING = 8
PER = HEADS // RING
TOK = 256
MESH = pl.DeviceIdType.MESH
DEAD = -1e30
EXPONENT = math.log2(math.e) / math.sqrt(SIZE)


def body(order_ref, mask_ref, q_ref, k_ref, v_ref, out_ref,
         qbuf, kv, obuf, mine, marks, bias, score,
         q_send, q_recv, y_send, y_recv, f_send, f_recv, m_send, m_recv, o_send, o_recv):
    inner = lax.axis_index("inner")
    outer = lax.axis_index("outer")
    x, lo, core = inner // 4, (inner // 2) % 2, inner % 2
    y, hi = outer // 4, outer % 4
    z = 2 * hi + lo
    home = lo == core

    def device(x_at, y_at, z_at, core_at):
        return (x_at * 4 + (z_at % 2) * 2 + core_at, y_at * 4 + z_at // 2)

    def owner(place, parity):
        return device(x, y, 2 * place + core, parity)

    up = device(x, (y + 1) % 4, z, core)
    down = device(x, (y + 3) % 4, z, core)
    after = device((x + core) % 4, y, z, 1 - core)
    before = device((x + 3 + core) % 4, y, z, 1 - core)

    barrier = pltpu.get_barrier_semaphore()
    for peer in (up, down, after, before):
        pl.semaphore_signal(barrier, inc=1, device_id=peer, device_id_type=MESH)
    for d in range(1, RING):
        pl.semaphore_signal(
            barrier, inc=1, device_id=device(x, y, (z + d) % RING, lo), device_id_type=MESH
        )

    @pl.when(jnp.logical_not(home))
    def _():
        pl.semaphore_signal(barrier, inc=1, device_id=device(x, y, z, lo), device_id_type=MESH)

    for place in range(4):
        for parity in range(2):
            @pl.when(jnp.logical_not(home & (place == hi) & (parity == core)))
            def _():
                pl.semaphore_signal(
                    barrier, inc=1, device_id=owner(place, parity), device_id_type=MESH
                )

    mine[...] = jnp.zeros_like(mine)
    for row in range(2):
        picked = order_ref[row] - 2 * (inner * 16 + outer)
        live = jnp.where(picked == 0, mask_ref[0:1, :], mask_ref[1:2, :])
        mine[row : row + 1, 0:30] = jnp.where(live > 0, 0.0, DEAD)

    pl.semaphore_wait(barrier, 20 - 2 * home.astype(jnp.int32))

    slot = 2 * hi + core

    def move(source, target, send, recv, to, local):
        if local is None:
            pltpu.make_async_remote_copy(
                src_ref=source, dst_ref=target, send_sem=send, recv_sem=recv,
                device_id=to, device_id_type=MESH,
            ).start()
        else:
            @pl.when(local)
            def _():
                pltpu.make_async_copy(source, target, recv).start()

            @pl.when(jnp.logical_not(local))
            def _():
                pltpu.make_async_remote_copy(
                    src_ref=source, dst_ref=target, send_sem=send, recv_sem=recv,
                    device_id=to, device_id_type=MESH,
                ).start()

    steps = (4, 3, 5, 2, 6, 1, 7, 0)
    for n, d in enumerate(steps):
        to = device(x, y, (z + d) % RING, lo)
        move(mine, marks.at[slot], m_send.at[n], m_recv.at[slot], to, home if d == 0 else None)

    def spread(h, carry):
        for t in range(3):
            for n, d in enumerate(steps):
                there = (z + d) % RING
                to = device(x, y, there, lo)
                cols = pl.ds(pl.multiple_of((there * PER + h) * SIZE, SIZE), SIZE)
                source = (k_ref, v_ref, q_ref)[t].at[:, cols]
                if t < 2:
                    target = kv.at[h, 1 + hi, 2 + core, t]
                else:
                    target = qbuf.at[h, slot]
                move(source, target, q_send.at[h, n, t], q_recv.at[h, slot, t], to,
                     home if d == 0 else None)
        return carry

    lax.fori_loop(0, PER, spread, 0)

    for s in range(RING):
        pltpu.make_async_copy(mine, marks.at[s], m_recv.at[s]).wait()

    def widen(s, carry):
        rows = marks[s]
        for w in range(30):
            bias[s, w] = jnp.broadcast_to(rows[:, w : w + 1], (8, SIZE))
        return carry

    lax.fori_loop(0, RING, widen, 0)

    def forward_copies(h, place):
        source = kv.at[h, place, pl.ds(2, 2)]
        return (
            pltpu.make_async_remote_copy(
                src_ref=source, dst_ref=kv.at[h, place, pl.ds(0, 2)],
                send_sem=f_send.at[h, place, 0], recv_sem=f_recv.at[h, place, 0],
                device_id=after, device_id_type=MESH),
            pltpu.make_async_remote_copy(
                src_ref=source, dst_ref=kv.at[h, place, pl.ds(4, 2)],
                send_sem=f_send.at[h, place, 1], recv_sem=f_recv.at[h, place, 1],
                device_id=before, device_id_type=MESH),
        )

    def edge_copy(h, side):
        return pltpu.make_async_remote_copy(
            src_ref=kv.at[h, 4 if side == 0 else 1, pl.ds(2, 2)],
            dst_ref=kv.at[h, 0 if side == 0 else 5, pl.ds(2, 2)],
            send_sem=y_send.at[h, side], recv_sem=y_recv.at[h, side],
            device_id=up if side == 0 else down, device_id_type=MESH)

    def send_out(h, j):
        place, parity = j // 2, j % 2
        cols = pl.ds(pl.multiple_of((z * PER + h) * SIZE, SIZE), SIZE)
        move(obuf.at[h, j], out_ref.at[:, cols], o_send.at[h, j], o_recv.at[h, z],
             owner(place, parity), home & (place == hi) & (parity == core))

    def attend(h, j):
        place, parity = j // 2, j % 2
        query = qbuf[h, j]
        top = jnp.full((TOK, SIZE), DEAD, jnp.float32)
        for s in range(15):
            step, side = s // 3, s % 3
            keyset = kv[h, place + side, parity + step, 0]
            raw = lax.dot_general(query, keyset, (((1,), (1,)), ((), ())),
                                  preferred_element_type=jnp.float32)
            for slot_at in range(2):
                w = 6 * step + 2 * side + slot_at
                part = raw[:, slot_at * SIZE : (slot_at + 1) * SIZE]
                upper = part[:SIZE] + bias[j, w, 0:1, :]
                lower = part[SIZE:] + bias[j, w, 1:2, :]
                part = jnp.concatenate([upper, lower], axis=0)
                score[2 * s + slot_at] = part
                top = jnp.maximum(top, part)
        top = jnp.max(top, axis=1, keepdims=True)
        total = jnp.zeros((TOK, SIZE), jnp.float32)
        numer = jnp.zeros((TOK, SIZE), jnp.float32)
        for s in range(15):
            step, side = s // 3, s % 3
            valset = kv[h, place + side, parity + step, 1]
            left = jnp.exp2((score[2 * s] - top) * EXPONENT)
            right = jnp.exp2((score[2 * s + 1] - top) * EXPONENT)
            total = total + left + right
            prob = jnp.concatenate([left, right], axis=1).astype(jnp.bfloat16)
            numer = numer + jnp.dot(prob, valset, preferred_element_type=jnp.float32)
        total = jnp.sum(total, axis=1, keepdims=True)
        obuf[h, j] = (numer / total).astype(jnp.bfloat16)

    def head(h, carry):
        for place in (3, 0, 1, 2):
            for parity in range(2):
                for t in range(2):
                    piece = kv.at[h, 1 + place, 2 + parity, t]
                    pltpu.make_async_copy(piece, piece, q_recv.at[h, 2 * place + parity, t]).wait()
            if place == 3:
                edge_copy(h, 0).start()
            if place == 0:
                edge_copy(h, 1).start()
            for copy in forward_copies(h, 1 + place):
                copy.start()
        for side in range(2):
            edge_copy(h, side).wait_recv()
            for copy in forward_copies(h, 5 * side):
                copy.start()
        for s in range(RING):
            pltpu.make_async_copy(qbuf.at[h, s], qbuf.at[h, s], q_recv.at[h, s, 2]).wait()

        @pl.when(h == PER - 1)
        def _():
            def early(n, carry):
                send_out(n // RING, n % RING)
                return carry

            lax.fori_loop(0, (PER - 1) * RING, early, 0)

        for place in range(6):
            for copy in forward_copies(h, place):
                copy.wait_recv()

        def one(j, carry):
            attend(h, j)

            @pl.when(h == PER - 1)
            def _():
                send_out(h, j)

            return carry

        lax.fori_loop(0, RING, one, 0)
        return carry

    lax.fori_loop(0, PER, head, 0)

    def finish(h, carry):
        for s in range(RING):
            cols = pl.ds(pl.multiple_of((s * PER + h) * SIZE, SIZE), SIZE)
            piece = out_ref.at[:, cols]
            pltpu.make_async_copy(piece, piece, o_recv.at[h, s]).wait()
        for n, d in enumerate(steps):
            for t in range(3):
                piece = qbuf.at[h, n]
                if d == 0:
                    @pl.when(jnp.logical_not(home))
                    def _():
                        pltpu.make_async_copy(piece, piece, q_send.at[h, n, t]).wait()
                else:
                    pltpu.make_async_copy(piece, piece, q_send.at[h, n, t]).wait()
        for side in range(2):
            edge_copy(h, side).wait_send()
        for place in range(6):
            for copy in forward_copies(h, place):
                copy.wait_send()
        for j in range(RING):
            place, parity = j // 2, j % 2

            @pl.when(jnp.logical_not(home & (place == hi) & (parity == core)))
            def _():
                piece = obuf.at[h, j]
                pltpu.make_async_copy(piece, piece, o_send.at[h, j]).wait()
        return carry

    lax.fori_loop(0, PER, finish, 0)
    for n, d in enumerate(steps):
        if d == 0:
            @pl.when(jnp.logical_not(home))
            def _():
                pltpu.make_async_copy(mine, mine, m_send.at[n]).wait()
        else:
            pltpu.make_async_copy(mine, mine, m_send.at[n]).wait()


def shards(queries, keys, values, frame_mask, query_order):
    anywhere = pl.BlockSpec(memory_space=pltpu.HBM)
    dma = pltpu.SemaphoreType.DMA
    return pl.pallas_call(
        body,
        out_shape=jax.ShapeDtypeStruct(queries.shape, queries.dtype),
        in_specs=[
            pl.BlockSpec(memory_space=pltpu.SMEM),
            pl.BlockSpec(memory_space=pltpu.VMEM),
            anywhere, anywhere, anywhere,
        ],
        out_specs=anywhere,
        scratch_shapes=[
            pltpu.VMEM((PER, RING, TOK, SIZE), jnp.bfloat16),
            pltpu.VMEM((PER, 6, 6, 2, TOK, SIZE), jnp.bfloat16),
            pltpu.VMEM((PER, RING, TOK, SIZE), jnp.bfloat16),
            pltpu.VMEM((8, SIZE), jnp.float32),
            pltpu.VMEM((RING, 8, SIZE), jnp.float32),
            pltpu.VMEM((RING, 30, 8, SIZE), jnp.float32),
            pltpu.VMEM((30, TOK, SIZE), jnp.float32),
            dma((PER, RING, 3)), dma((PER, RING, 3)),
            dma((PER, 2)), dma((PER, 2)),
            dma((PER, 6, 2)), dma((PER, 6, 2)),
            dma((RING,)), dma((RING,)),
            dma((PER, RING)), dma((PER, RING)),
        ],
        compiler_params=pltpu.CompilerParams(
            collective_id=0, has_side_effects=True, vmem_limit_bytes=48 << 20
        ),
        cost_estimate=pl.CostEstimate(
            flops=12_000_000_000, bytes_accessed=7_000_000, transcendentals=24_000_000
        ),
        name="ring_attention",
    )(query_order, frame_mask, queries, keys, values)


def solution(mesh):
    placed = (
        P(("inner", "outer"), None),
        P(("inner", "outer"), None),
        P(("inner", "outer"), None),
        P(("inner", "outer"), None),
        P(("inner", "outer")),
    )
    return jax.shard_map(
        shards, mesh=mesh, in_specs=placed, out_specs=P(("inner", "outer"), None), check_vma=False
    )
```

time: 446 us -> 158 us (0.35)
  the two profiles are of different devices: /device:TPU:26 before, /device:TPU:3 now
where the time goes in v1:
time: 158 us
  Pallas kernels  153 us (97%)
  local copies, waits for them, and re-layouts  5.29 us (3%)
    pallas_call x1, Pallas kernels, shards(): pl.pallas_call(body, out_shape=jax.ShapeDtypeStruct(queries.shape, querie...  153 us
    unnamed x9, local copies, waits for them, and re-layouts  5.29 us

profile of v1, /device:TPU:3, one launch (start us, length us, event | category | flops | bytes accessed | tf_op | source)
XLA Modules:
  0.0 157.8 jit_solution(18116435234959694926)
XLA Ops:
  0.0 0.0 copy-start
  0.0 1.4 copy-done
  1.4 0.0 copy-start.1
  1.4 1.4 copy-done.1
  2.8 0.0 copy-start.2
  2.8 0.7 copy-done.2
  3.5 0.0 copy-start.3
  3.5 0.7 copy-done.3
  4.2 152.5 %ring_attention.1 = bf16[256,3072]{1,0:T(8,128)(2,1)S(1)} custom-call(s32[2]{0:T(128)S(1)} %copy-done.3, s32[2,30]{1,0:T(2,128)S(1)} %copy-done.2, bf16[256,3072]{1,0:T(8,128)(2,1)S(1)} %copy-done, bf16[256,3072]{1,0:T(8,128)(2,1)S(1)} %copy-done.1, bf16[256,3072]{1,0:T(8,128)(2,1)} %v_ref.1), custom_call_target="tpu_custom_call" | custom-call | flops 12000000000 | bytes 7000000 | tf_op jit(solution)/shard_map/ring_attention/pallas_call | solution.py:265
  156.7 1.1 copy.7
Async XLA Ops:
  0.0 1.4 copy-start
  1.4 1.4 copy-start.1
  2.8 0.7 copy-start.2
  3.5 0.7 copy-start.3

commit v2 on v1

--- a/solution.py
+++ b/solution.py
@@ -39,8 +39,6 @@
     before = device((x + 3 + core) % 4, y, z, 1 - core)
 
     barrier = pltpu.get_barrier_semaphore()
-    for peer in (up, down, after, before):
-        pl.semaphore_signal(barrier, inc=1, device_id=peer, device_id_type=MESH)
     for d in range(1, RING):
         pl.semaphore_signal(
             barrier, inc=1, device_id=device(x, y, (z + d) % RING, lo), device_id_type=MESH
@@ -51,12 +49,11 @@
         pl.semaphore_signal(barrier, inc=1, device_id=device(x, y, z, lo), device_id_type=MESH)
 
     for place in range(4):
-        for parity in range(2):
-            @pl.when(jnp.logical_not(home & (place == hi) & (parity == core)))
-            def _():
-                pl.semaphore_signal(
-                    barrier, inc=1, device_id=owner(place, parity), device_id_type=MESH
-                )
+        pl.semaphore_signal(
+            barrier, inc=1, device_id=owner(place, 1 - lo), device_id_type=MESH
+        )
+    for peer in (up, down, device((x + 2 * core + 3) % 4, y, z, 1 - core)):
+        pl.semaphore_signal(barrier, inc=1, device_id=peer, device_id_type=MESH)
 
     mine[...] = jnp.zeros_like(mine)
     for row in range(2):
@@ -64,7 +61,7 @@
         live = jnp.where(picked == 0, mask_ref[0:1, :], mask_ref[1:2, :])
         mine[row : row + 1, 0:30] = jnp.where(live > 0, 0.0, DEAD)
 
-    pl.semaphore_wait(barrier, 20 - 2 * home.astype(jnp.int32))
+    pl.semaphore_wait(barrier, 15 - home.astype(jnp.int32))
 
     slot = 2 * hi + core
 
@@ -87,37 +84,33 @@
                 ).start()
 
     steps = (4, 3, 5, 2, 6, 1, 7, 0)
+    def spread(h, t):
+        for n, d in enumerate(steps):
+            there = (z + d) % RING
+            to = device(x, y, there, lo)
+            cols = pl.ds(pl.multiple_of((there * PER + h) * SIZE, SIZE), SIZE)
+            source = (k_ref, v_ref, q_ref)[t].at[:, cols]
+            if t < 2:
+                target = kv.at[h, 1 + hi, 2 + core, t]
+            else:
+                target = qbuf.at[h, slot]
+            move(source, target, q_send.at[h, n, t], q_recv.at[h, slot, t], to,
+                 home if d == 0 else None)
+
+    def spread_kv(h, carry):
+        spread(h, 0)
+        spread(h, 1)
+        return carry
+
+    def spread_q(h, carry):
+        spread(h, 2)
+        return carry
+
+    lax.fori_loop(0, PER, spread_kv, 0)
     for n, d in enumerate(steps):
         to = device(x, y, (z + d) % RING, lo)
         move(mine, marks.at[slot], m_send.at[n], m_recv.at[slot], to, home if d == 0 else None)
-
-    def spread(h, carry):
-        for t in range(3):
-            for n, d in enumerate(steps):
-                there = (z + d) % RING
-                to = device(x, y, there, lo)
-                cols = pl.ds(pl.multiple_of((there * PER + h) * SIZE, SIZE), SIZE)
-                source = (k_ref, v_ref, q_ref)[t].at[:, cols]
-                if t < 2:
-                    target = kv.at[h, 1 + hi, 2 + core, t]
-                else:
-                    target = qbuf.at[h, slot]
-                move(source, target, q_send.at[h, n, t], q_recv.at[h, slot, t], to,
-                     home if d == 0 else None)
-        return carry
-
-    lax.fori_loop(0, PER, spread, 0)
-
-    for s in range(RING):
-        pltpu.make_async_copy(mine, marks.at[s], m_recv.at[s]).wait()
-
-    def widen(s, carry):
-        rows = marks[s]
-        for w in range(30):
-            bias[s, w] = jnp.broadcast_to(rows[:, w : w + 1], (8, SIZE))
-        return carry
-
-    lax.fori_loop(0, RING, widen, 0)
+    lax.fori_loop(0, PER, spread_q, 0)
 
     def forward_copies(h, place):
         source = kv.at[h, place, pl.ds(2, 2)]
@@ -176,8 +169,9 @@
         total = jnp.sum(total, axis=1, keepdims=True)
         obuf[h, j] = (numer / total).astype(jnp.bfloat16)
 
-    def head(h, carry):
-        for place in (3, 0, 1, 2):
+    def gather(h, carry):
+        for n in range(4):
+            place = (3, 0, 1, 2)[n]
             for parity in range(2):
                 for t in range(2):
                     piece = kv.at[h, 1 + place, 2 + parity, t]
@@ -192,40 +186,51 @@
             edge_copy(h, side).wait_recv()
             for copy in forward_copies(h, 5 * side):
                 copy.start()
-        for s in range(RING):
-            pltpu.make_async_copy(qbuf.at[h, s], qbuf.at[h, s], q_recv.at[h, s, 2]).wait()
-
-        @pl.when(h == PER - 1)
-        def _():
-            def early(n, carry):
-                send_out(n // RING, n % RING)
-                return carry
-
-            lax.fori_loop(0, (PER - 1) * RING, early, 0)
-
+        return carry
+
+    lax.fori_loop(0, PER, gather, 0)
+
+    for s in range(RING):
+        pltpu.make_async_copy(mine, marks.at[s], m_recv.at[s]).wait()
+
+    def widen(s, carry):
+        rows = marks[s]
+        for w in range(30):
+            bias[s, w] = jnp.broadcast_to(rows[:, w : w + 1], (2, SIZE))
+        return carry
+
+    lax.fori_loop(0, RING, widen, 0)
+
+    def head(h, carry):
         for place in range(6):
             for copy in forward_copies(h, place):
                 copy.wait_recv()
 
-        def one(j, carry):
+        def one(n, carry):
+            rank = n // 2
+            even = jnp.where(rank == 0, 4, jnp.where(rank == 1, 2, jnp.where(rank == 2, 6, 0)))
+            odd = jnp.where(rank == 0, 3, jnp.where(rank == 1, 5, jnp.where(rank == 2, 1, 7)))
+            away = jnp.where(home, even, odd)
+            j = 2 * (((z - away + RING) % RING) // 2) + n % 2
+            pltpu.make_async_copy(qbuf.at[h, j], qbuf.at[h, j], q_recv.at[h, j, 2]).wait()
             attend(h, j)
-
-            @pl.when(h == PER - 1)
+            send_out(h, j)
+            return carry
+
+        lax.fori_loop(0, RING, one, 0)
+        return carry
+
+    lax.fori_loop(0, PER, head, 0)
+
+    for n, d in enumerate(steps):
+        if d == 0:
+            @pl.when(jnp.logical_not(home))
             def _():
-                send_out(h, j)
-
-            return carry
-
-        lax.fori_loop(0, RING, one, 0)
-        return carry
-
-    lax.fori_loop(0, PER, head, 0)
-
-    def finish(h, carry):
-        for s in range(RING):
-            cols = pl.ds(pl.multiple_of((s * PER + h) * SIZE, SIZE), SIZE)
-            piece = out_ref.at[:, cols]
-            pltpu.make_async_copy(piece, piece, o_recv.at[h, s]).wait()
+                pltpu.make_async_copy(mine, mine, m_send.at[n]).wait()
+        else:
+            pltpu.make_async_copy(mine, mine, m_send.at[n]).wait()
+
+    def inputs_left(h, carry):
         for n, d in enumerate(steps):
             for t in range(3):
                 piece = qbuf.at[h, n]
@@ -240,6 +245,11 @@
         for place in range(6):
             for copy in forward_copies(h, place):
                 copy.wait_send()
+        return carry
+
+    lax.fori_loop(0, PER, inputs_left, 0)
+
+    def outputs_left(h, carry):
         for j in range(RING):
             place, parity = j // 2, j % 2
 
@@ -247,24 +257,21 @@
             def _():
                 piece = obuf.at[h, j]
                 pltpu.make_async_copy(piece, piece, o_send.at[h, j]).wait()
-        return carry
-
-    lax.fori_loop(0, PER, finish, 0)
-    for n, d in enumerate(steps):
-        if d == 0:
-            @pl.when(jnp.logical_not(home))
-            def _():
-                pltpu.make_async_copy(mine, mine, m_send.at[n]).wait()
-        else:
-            pltpu.make_async_copy(mine, mine, m_send.at[n]).wait()
+        for s in range(RING):
+            cols = pl.ds(pl.multiple_of((s * PER + h) * SIZE, SIZE), SIZE)
+            piece = out_ref.at[:, cols]
+            pltpu.make_async_copy(piece, piece, o_recv.at[h, s]).wait()
+        return carry
+
+    lax.fori_loop(0, PER, outputs_left, 0)
 
 
 def shards(queries, keys, values, frame_mask, query_order):
-    anywhere = pl.BlockSpec(memory_space=pltpu.HBM)
+    anywhere = pl.BlockSpec(memory_space=pl.ANY)
     dma = pltpu.SemaphoreType.DMA
     return pl.pallas_call(
         body,
-        out_shape=jax.ShapeDtypeStruct(queries.shape, queries.dtype),
+        out_shape=pltpu.VMEM(queries.shape, queries.dtype),
         in_specs=[
             pl.BlockSpec(memory_space=pltpu.SMEM),
             pl.BlockSpec(memory_space=pltpu.VMEM),
@@ -275,9 +282,9 @@
             pltpu.VMEM((PER, RING, TOK, SIZE), jnp.bfloat16),
             pltpu.VMEM((PER, 6, 6, 2, TOK, SIZE), jnp.bfloat16),
             pltpu.VMEM((PER, RING, TOK, SIZE), jnp.bfloat16),
-            pltpu.VMEM((8, SIZE), jnp.float32),
-            pltpu.VMEM((RING, 8, SIZE), jnp.float32),
-            pltpu.VMEM((RING, 30, 8, SIZE), jnp.float32),
+            pltpu.VMEM((2, SIZE), jnp.float32),
+            pltpu.VMEM((RING, 2, SIZE), jnp.float32),
+            pltpu.VMEM((RING, 30, 2, SIZE), jnp.float32),
             pltpu.VMEM((30, TOK, SIZE), jnp.float32),
             dma((PER, RING, 3)), dma((PER, RING, 3)),
             dma((PER, 2)), dma((PER, 2)),
@@ -286,7 +293,7 @@
             dma((PER, RING)), dma((PER, RING)),
         ],
         compiler_params=pltpu.CompilerParams(
-            collective_id=0, has_side_effects=True, vmem_limit_bytes=48 << 20
+            collective_id=0, has_side_effects=True, vmem_limit_bytes=62 << 20
         ),
         cost_estimate=pl.CostEstimate(
             flops=12_000_000_000, bytes_accessed=7_000_000, transcendentals=24_000_000

time: 158 us -> 151 us (0.956)
  local copies, waits for them, and re-layouts: 5.29 us -> 1.15 us
  Pallas kernels: 153 us -> 149 us
    unnamed x9 -> x1, local copies, waits for them, and re-layouts: 5.29 us -> 1.15 us
    pallas_call x1, Pallas kernels: 153 us -> 149 us  [shards(): pl.pallas_call(body, out_shape=pltpu.VMEM(queries.shape, queries.dtype),...]
where the time goes in v2:
time: 151 us; the launch traced here: 150 us
  Pallas kernels  149 us (99%)
    pallas_call x1, Pallas kernels, shards(): pl.pallas_call(body, out_shape=pltpu.VMEM(queries.shape, queries.dtype),...  149 us

profile of v2, /device:TPU:3, one launch (start us, length us, event | category | flops | bytes accessed | tf_op | source)
XLA Modules:
  0.0 149.7 jit_solution(5209235423335842308)
XLA Ops:
  0.0 148.5 %ring_attention.1 = bf16[256,3072]{1,0:T(8,128)(2,1)S(1)} custom-call(s32[2]{0:T(128)} %order_ref.1, s32[2,30]{1,0:T(2,128)} %mask_ref.1, bf16[256,3072]{1,0:T(8,128)(2,1)} %q_ref.1, bf16[256,3072]{1,0:T(8,128)(2,1)} %k_ref.1, bf16[256,3072]{1,0:T(8,128)(2,1)} %v_ref.1), custom_call_target="tpu_custom_call" | custom-call | flops 12000000000 | bytes 7000000 | tf_op jit(solution)/shard_map/ring_attention/pallas_call | solution.py:272
  148.5 1.1 copy.7

commit v3 on v2

--- a/solution.py
+++ b/solution.py
@@ -211,7 +211,10 @@
             even = jnp.where(rank == 0, 4, jnp.where(rank == 1, 2, jnp.where(rank == 2, 6, 0)))
             odd = jnp.where(rank == 0, 3, jnp.where(rank == 1, 5, jnp.where(rank == 2, 1, 7)))
             away = jnp.where(home, even, odd)
-            j = 2 * (((z - away + RING) % RING) // 2) + n % 2
+            ranked = ((z - away + RING) % RING) // 2
+            place = jnp.where(h == PER - 1, rank, ranked)
+            flip = jnp.where(rank == 1, 0, 1)
+            j = 2 * place + (n + flip) % 2
             pltpu.make_async_copy(qbuf.at[h, j], qbuf.at[h, j], q_recv.at[h, j, 2]).wait()
             attend(h, j)
             send_out(h, j)

time: 151 us -> 149 us (0.987); the launches traced: 150 us -> 146 us
  Pallas kernels: 149 us -> 145 us
    pallas_call x1, Pallas kernels: 149 us -> 145 us  [shards(): pl.pallas_call(body, out_shape=pltpu.VMEM(queries.shape, queries.dtype),...]
where the time goes in v3:
time: 149 us; the launch traced here: 146 us
  Pallas kernels  145 us (97%)
    pallas_call x1, Pallas kernels, shards(): pl.pallas_call(body, out_shape=pltpu.VMEM(queries.shape, queries.dtype),...  145 us

profile of v3, /device:TPU:3, one launch (start us, length us, event | category | flops | bytes accessed | tf_op | source)
XLA Modules:
  0.0 146.1 jit_solution(8337618924770560266)
XLA Ops:
  0.0 145.0 %ring_attention.1 = bf16[256,3072]{1,0:T(8,128)(2,1)S(1)} custom-call(s32[2]{0:T(128)} %order_ref.1, s32[2,30]{1,0:T(2,128)} %mask_ref.1, bf16[256,3072]{1,0:T(8,128)(2,1)} %q_ref.1, bf16[256,3072]{1,0:T(8,128)(2,1)} %k_ref.1, bf16[256,3072]{1,0:T(8,128)(2,1)} %v_ref.1), custom_call_target="tpu_custom_call" | custom-call | flops 12000000000 | bytes 7000000 | tf_op jit(solution)/shard_map/ring_attention/pallas_call | solution.py:275
  145.0 1.1 copy.7

commit v4 on v3

--- a/solution.py
+++ b/solution.py
@@ -19,7 +19,7 @@
 
 def body(order_ref, mask_ref, q_ref, k_ref, v_ref, out_ref,
          qbuf, kv, obuf, mine, marks, bias, score,
-         q_send, q_recv, y_send, y_recv, f_send, f_recv, m_send, m_recv, o_send, o_recv):
+         i_send, kv_recv, q_recv, y_send, y_recv, f_send, f_recv, m_send, m_recv, o_send, o_recv):
     inner = lax.axis_index("inner")
     outer = lax.axis_index("outer")
     x, lo, core = inner // 4, (inner // 2) % 2, inner % 2
@@ -85,7 +85,7 @@
 
     steps = (4, 3, 5, 2, 6, 1, 7, 0)
     def spread(h, t):
-        for n, d in enumerate(steps):
+        for d in steps:
             there = (z + d) % RING
             to = device(x, y, there, lo)
             cols = pl.ds(pl.multiple_of((there * PER + h) * SIZE, SIZE), SIZE)
@@ -94,8 +94,8 @@
                 target = kv.at[h, 1 + hi, 2 + core, t]
             else:
                 target = qbuf.at[h, slot]
-            move(source, target, q_send.at[h, n, t], q_recv.at[h, slot, t], to,
-                 home if d == 0 else None)
+            arrived = kv_recv.at[h] if t < 2 else q_recv.at[h]
+            move(source, target, i_send.at[t], arrived, to, home if d == 0 else None)
 
     def spread_kv(h, carry):
         spread(h, 0)
@@ -107,9 +107,9 @@
         return carry
 
     lax.fori_loop(0, PER, spread_kv, 0)
-    for n, d in enumerate(steps):
+    for d in steps:
         to = device(x, y, (z + d) % RING, lo)
-        move(mine, marks.at[slot], m_send.at[n], m_recv.at[slot], to, home if d == 0 else None)
+        move(mine, marks.at[slot], m_send, m_recv, to, home if d == 0 else None)
     lax.fori_loop(0, PER, spread_q, 0)
 
     def forward_copies(h, place):
@@ -117,11 +117,11 @@
         return (
             pltpu.make_async_remote_copy(
                 src_ref=source, dst_ref=kv.at[h, place, pl.ds(0, 2)],
-                send_sem=f_send.at[h, place, 0], recv_sem=f_recv.at[h, place, 0],
+                send_sem=f_send.at[h], recv_sem=f_recv.at[h, 0],
                 device_id=after, device_id_type=MESH),
             pltpu.make_async_remote_copy(
                 src_ref=source, dst_ref=kv.at[h, place, pl.ds(4, 2)],
-                send_sem=f_send.at[h, place, 1], recv_sem=f_recv.at[h, place, 1],
+                send_sem=f_send.at[h], recv_sem=f_recv.at[h, 1],
                 device_id=before, device_id_type=MESH),
         )
 
@@ -129,13 +129,13 @@
         return pltpu.make_async_remote_copy(
             src_ref=kv.at[h, 4 if side == 0 else 1, pl.ds(2, 2)],
             dst_ref=kv.at[h, 0 if side == 0 else 5, pl.ds(2, 2)],
-            send_sem=y_send.at[h, side], recv_sem=y_recv.at[h, side],
+            send_sem=y_send, recv_sem=y_recv.at[h, side],
             device_id=up if side == 0 else down, device_id_type=MESH)
 
     def send_out(h, j):
         place, parity = j // 2, j % 2
         cols = pl.ds(pl.multiple_of((z * PER + h) * SIZE, SIZE), SIZE)
-        move(obuf.at[h, j], out_ref.at[:, cols], o_send.at[h, j], o_recv.at[h, z],
+        move(obuf.at[h, j], out_ref.at[:, cols], o_send, o_recv,
              owner(place, parity), home & (place == hi) & (parity == core))
 
     def attend(h, j):
@@ -169,18 +169,15 @@
         total = jnp.sum(total, axis=1, keepdims=True)
         obuf[h, j] = (numer / total).astype(jnp.bfloat16)
 
+    def settle(piece, sem):
+        pltpu.make_async_copy(piece, piece, sem).wait()
+
     def gather(h, carry):
-        for n in range(4):
-            place = (3, 0, 1, 2)[n]
-            for parity in range(2):
-                for t in range(2):
-                    piece = kv.at[h, 1 + place, 2 + parity, t]
-                    pltpu.make_async_copy(piece, piece, q_recv.at[h, 2 * place + parity, t]).wait()
-            if place == 3:
-                edge_copy(h, 0).start()
-            if place == 0:
-                edge_copy(h, 1).start()
-            for copy in forward_copies(h, 1 + place):
+        settle(kv.at[h, pl.ds(1, 4), pl.ds(2, 2)], kv_recv.at[h])
+        for side in range(2):
+            edge_copy(h, side).start()
+        for place in range(1, 5):
+            for copy in forward_copies(h, place):
                 copy.start()
         for side in range(2):
             edge_copy(h, side).wait_recv()
@@ -190,8 +187,7 @@
 
     lax.fori_loop(0, PER, gather, 0)
 
-    for s in range(RING):
-        pltpu.make_async_copy(mine, marks.at[s], m_recv.at[s]).wait()
+    settle(marks, m_recv)
 
     def widen(s, carry):
         rows = marks[s]
@@ -202,9 +198,9 @@
     lax.fori_loop(0, RING, widen, 0)
 
     def head(h, carry):
-        for place in range(6):
-            for copy in forward_copies(h, place):
-                copy.wait_recv()
+        for side in range(2):
+            settle(kv.at[h, :, pl.ds(4 * side, 2)], f_recv.at[h, side])
+        settle(qbuf.at[h], q_recv.at[h])
 
         def one(n, carry):
             rank = n // 2
@@ -215,7 +211,6 @@
             place = jnp.where(h == PER - 1, rank, ranked)
             flip = jnp.where(rank == 1, 0, 1)
             j = 2 * place + (n + flip) % 2
-            pltpu.make_async_copy(qbuf.at[h, j], qbuf.at[h, j], q_recv.at[h, j, 2]).wait()
             attend(h, j)
             send_out(h, j)
             return carry
@@ -225,48 +220,23 @@
 
     lax.fori_loop(0, PER, head, 0)
 
-    for n, d in enumerate(steps):
-        if d == 0:
-            @pl.when(jnp.logical_not(home))
-            def _():
-                pltpu.make_async_copy(mine, mine, m_send.at[n]).wait()
-        else:
-            pltpu.make_async_copy(mine, mine, m_send.at[n]).wait()
-
-    def inputs_left(h, carry):
-        for n, d in enumerate(steps):
-            for t in range(3):
-                piece = qbuf.at[h, n]
-                if d == 0:
-                    @pl.when(jnp.logical_not(home))
-                    def _():
-                        pltpu.make_async_copy(piece, piece, q_send.at[h, n, t]).wait()
-                else:
-                    pltpu.make_async_copy(piece, piece, q_send.at[h, n, t]).wait()
-        for side in range(2):
-            edge_copy(h, side).wait_send()
-        for place in range(6):
-            for copy in forward_copies(h, place):
-                copy.wait_send()
-        return carry
-
-    lax.fori_loop(0, PER, inputs_left, 0)
-
-    def outputs_left(h, carry):
-        for j in range(RING):
-            place, parity = j // 2, j % 2
-
-            @pl.when(jnp.logical_not(home & (place == hi) & (parity == core)))
-            def _():
-                piece = obuf.at[h, j]
-                pltpu.make_async_copy(piece, piece, o_send.at[h, j]).wait()
-        for s in range(RING):
-            cols = pl.ds(pl.multiple_of((s * PER + h) * SIZE, SIZE), SIZE)
-            piece = out_ref.at[:, cols]
-            pltpu.make_async_copy(piece, piece, o_recv.at[h, s]).wait()
-        return carry
-
-    lax.fori_loop(0, PER, outputs_left, 0)
+    def settle_sent(buffer, few, sem):
+        @pl.when(home)
+        def _():
+            settle(few, sem)
+
+        @pl.when(jnp.logical_not(home))
+        def _():
+            settle(buffer, sem)
+
+    settle_sent(marks, marks.at[pl.ds(0, RING - 1)], m_send)
+    for t in range(3):
+        settle_sent(qbuf, qbuf.at[:, pl.ds(0, RING - 1)], i_send.at[t])
+    settle(qbuf, y_send)
+    for h in range(PER):
+        settle(kv.at[h, :, pl.ds(0, 4)], f_send.at[h])
+    settle_sent(obuf, obuf.at[:, pl.ds(0, RING - 1)], o_send)
+    settle(out_ref, o_recv)
 
 
 def shards(queries, keys, values, frame_mask, query_order):
@@ -289,11 +259,11 @@
             pltpu.VMEM((RING, 2, SIZE), jnp.float32),
             pltpu.VMEM((RING, 30, 2, SIZE), jnp.float32),
             pltpu.VMEM((30, TOK, SIZE), jnp.float32),
-            dma((PER, RING, 3)), dma((PER, RING, 3)),
-            dma((PER, 2)), dma((PER, 2)),
-            dma((PER, 6, 2)), dma((PER, 6, 2)),
-            dma((RING,)), dma((RING,)),
-            dma((PER, RING)), dma((PER, RING)),
+            dma((3,)), dma((PER,)), dma((PER,)),
+            dma, dma((PER, 2)),
+            dma((PER,)), dma((PER, 2)),
+            dma, dma,
+            dma, dma,
         ],
         compiler_params=pltpu.CompilerParams(
             collective_id=0, has_side_effects=True, vmem_limit_bytes=62 << 20

time: 149 us -> 148 us (level); the launches traced: 146 us -> 147 us
  no operation moved by 1% of the time
where the time goes in v4:
time: 148 us; the launch traced here: 147 us
  Pallas kernels  146 us (99%)
    pallas_call x1, Pallas kernels, shards(): pl.pallas_call(body, out_shape=pltpu.VMEM(queries.shape, queries.dtype),...  146 us

profile of v4, /device:TPU:3, one launch (start us, length us, event | category | flops | bytes accessed | tf_op | source)
XLA Modules:
  0.0 146.8 jit_solution(16998416289618250365)
XLA Ops:
  0.0 145.7 %ring_attention.1 = bf16[256,3072]{1,0:T(8,128)(2,1)S(1)} custom-call(s32[2]{0:T(128)} %order_ref.1, s32[2,30]{1,0:T(2,128)} %mask_ref.1, bf16[256,3072]{1,0:T(8,128)(2,1)} %q_ref.1, bf16[256,3072]{1,0:T(8,128)(2,1)} %k_ref.1, bf16[256,3072]{1,0:T(8,128)(2,1)} %v_ref.1), custom_call_target="tpu_custom_call" | custom-call | flops 12000000000 | bytes 7000000 | tf_op jit(solution)/shard_map/ring_attention/pallas_call | solution.py:245
  145.7 1.1 copy.7
